TPU v7x, 32 devices: a whole 2x2x4 slice. The times are simulated.
32 devices in a mesh: outer: 8 (over y, x, core), inner: 4 (over z).
Axes of the slice: x: 2, y: 2, z: 4, core: 2. Of those that a mesh axis runs over, the one named last changes fastest.
Arguments:
- queries: bfloat16 [4096, 768], P(('outer', 'inner')), may hold values from -5.5 to 5.5
- keys: bfloat16 [4096, 128], P(('outer', 'inner')), may hold values from -5.5 to 5.5
- values: bfloat16 [4096, 128], P(('outer', 'inner')), may hold values from -6 to 6
- grad_out: bfloat16 [4096, 768], P(('outer', 'inner')), may hold values from -96 to 96
- span_slot: int32 [64], replicated, may hold values from 0 to 63, as said below
Outputs:
- grad_queries: bfloat16 [4096, 768], P(('outer', 'inner'))
- grad_keys: bfloat16 [4096, 128], P(('outer', 'inner'))
- grad_values: bfloat16 [4096, 128], P(('outer', 'inner'))
Inputs may be any that keep to these rules, and one draw needn't show every extreme that they name: `span_slot`: slots 2 d and 2 d + 1 hold spans c and 63 - c for some c below 32; every span is held once.
All inputs are finite; a program needn't handle non-finite values.
Results may differ from a plain program's by a relative error of at most 0.0074.
Values may be sent and summed in bfloat16 or wider, within the bound.
A program may use at most 128 MiB of HBM per device.

v0:
```python
import functools
import math

import jax
import jax.numpy as jnp
import numpy as np
from jax import lax
from jax.experimental import pallas as pl
from jax.experimental.pallas import tpu as pltpu
from jax.sharding import PartitionSpec as P

NEG_FILL = -1e30
LOG2E = math.log2(math.e)
MIB = 1024 * 1024
MESH = pl.DeviceIdType.MESH


def bits_of(outer, inner):
    near = [("inner", b) for b in range(inner.bit_length() - 1)]
    chips = [("outer", b) for b in range(1, outer.bit_length() - 1)]
    core = [("outer", 0)]
    return near + chips + core, near[::-1] + chips[::-1] + core


def place_of(order, o, i):
    place = 0
    for at, (axis, b) in enumerate(order):
        place = place + (((o if axis == "outer" else i) // 2**b) % 2) * 2**at
    return place


def partner_of(axis, b, o, i):
    if axis == "outer":
        return (o + (1 - 2 * ((o // 2**b) % 2)) * 2**b, i)
    return (o, i + (1 - 2 * ((i // 2**b) % 2)) * 2**b)


def greet(order, o, i):
    barrier = pltpu.get_barrier_semaphore()
    for axis, b in order:
        pl.semaphore_signal(barrier, inc=1, device_id=partner_of(axis, b, o, i), device_id_type=MESH)
    pl.semaphore_wait(barrier, len(order))


def flip(place, step):
    return place + (1 - 2 * ((place // 2**step) % 2)) * 2**step


def units(place, near):
    return [(place, 0)] + [(flip(place, step), step) for step in range(near)]


def lines(place, near, step):
    if step == near:
        return [place]
    return lines(flip(place, step - 1), near, step - 1) + lines(place, near, step - 1)


def moves_of(near, chips):
    return near + (near + 1) * (2**chips - 1) + chips + 1


def gather_kernel(orders, k_in, v_in, k_out, v_out, send, recv, own):
    o, i = lax.axis_index("outer"), lax.axis_index("inner")
    rows = k_in.shape[0]
    chain = len(orders[0]) - 1
    near = sum(axis == "inner" for axis, _ in orders[0])
    places = [place_of(order, o, i) for order in orders]
    outs = (k_out, v_out)

    def span_of(place, step):
        size = rows * 2**step
        return pl.ds(pl.multiple_of((place // 2**step) * size, size), size)

    owned = [
        pltpu.make_async_copy((k_in, v_in)[a], outs[a].at[span_of(places[a], 0), :], own.at[a]) for a in (0, 1)
    ]
    for copy in owned:
        copy.start()
    greet(orders[0], o, i)
    copies, waited = ({}, {}), set()

    def begin(a, name, part, bit):
        part = outs[a].at[part, :]
        at = len(copies[a])
        copies[a][name] = pltpu.make_async_remote_copy(
            src_ref=part, dst_ref=part, send_sem=send.at[a, at], recv_sem=recv.at[a, at],
            device_id=partner_of(*bit, o, i), device_id_type=MESH)
        copies[a][name].start()

    def arrive(a, name):
        copies[a][name].wait_recv()
        waited.add((a, name))

    def spread(a, path, unit, step):
        place = places[a]
        for bit in path:
            place = flip(place, bit)
        where, size = units(place, near)[unit]
        for later in range(step, chain):
            begin(a, (path + (later,), unit), span_of(where, size), orders[a][later])

    paths = [()]
    for bit in range(near, chain):
        paths = paths + [path + (bit,) for path in paths]
    for a in (0, 1):
        owned[a].wait()
        begin(a, 0, span_of(places[a], 0), orders[a][0])
    for a in (0, 1):
        spread(a, (), 0, near)
    for unit in range(near + 1):
        if unit:
            for a in (0, 1):
                arrive(a, unit - 1)
                if unit < near:
                    begin(a, unit, span_of(places[a], unit), orders[a][unit])
                spread(a, (), unit, near)
                if unit == near:
                    begin(a, "core", span_of(places[a], near), orders[a][chain])
        for path in paths[1:]:
            if path[-1] < chain - 1:
                for a in (0, 1):
                    arrive(a, (path, unit))
                    spread(a, path, unit, path[-1] + 1)
    for bit in range(near, chain):
        for a in (0, 1):
            for unit in range(near + 1):
                for path in paths[1:]:
                    if path[-1] == bit and (a, (path, unit)) not in waited:
                        arrive(a, (path, unit))
            begin(a, ("core", bit), span_of(flip(places[a], bit), bit), orders[a][chain])
    for a in (0, 1):
        for name, copy in copies[a].items():
            copy.wait_send()
            if (a, name) not in waited:
                copy.wait_recv()


def scatter_kernel(orders, k_in, v_in, k_out, v_out, k_acc, v_acc, k_got, v_got, k_core, v_core, send, recv):
    o, i = lax.axis_index("outer"), lax.axis_index("inner")
    rows = k_out.shape[0]
    chain = len(orders[0]) - 1
    near = sum(axis == "inner" for axis, _ in orders[0])
    greet(orders[0], o, i)
    half = 2**chain
    ins, outs, accs = (k_in, v_in), (k_out, v_out), (k_acc, v_acc)
    gots, cores = (k_got, v_got), (k_core, v_core)
    full = [place_of(order, o, i) for order in orders]
    places = [place % half for place in full]
    sides = [place // half for place in full]
    copies = ({}, {})

    def spot(place, step, offset=0):
        size = rows * 2**step
        return pl.ds(pl.multiple_of((place // 2**step) * size + offset, size), size)

    def begin(a, name, src, dst, bit):
        at = len(copies[a])
        copies[a][name] = pltpu.make_async_remote_copy(
            src_ref=src, dst_ref=dst, send_sem=send.at[a, at], recv_sem=recv.at[a, at],
            device_id=partner_of(*bit, o, i), device_id_type=MESH)
        copies[a][name].start()

    def landing(step, place, size):
        return spot(place % 2**step, size, rows * 2**step)

    def forward(a, step, name, place, size):
        begin(a, (step,) + name, accs[a].at[spot(place, size), :], gots[a].at[landing(step, place, size), :],
              orders[a][step])

    def add(a, step, place, size):
        got = gots[a][landing(step, place, size), :]
        return accs[a][spot(place, size), :].astype(jnp.float32) + got.astype(jnp.float32)

    def pieces(a):
        return [(flip(places[a], step), step) for step in range(chain - 1, near - 1, -1)] + [(places[a], near)]

    def join(a, which):
        place, step = pieces(a)[which]
        copies[a]["core", which].wait_recv()
        mine = ins[a][spot(place, step, sides[a] * half * rows), :]
        total = mine.astype(jnp.float32) + cores[a][spot(place, step), :].astype(jnp.float32)
        accs[a][spot(place, step), :] = total.astype(jnp.bfloat16)

    for which in range(chain - near + 1):
        for a in (0, 1):
            place, step = pieces(a)[which]
            begin(a, ("core", which), ins[a].at[spot(place, step, (1 - sides[a]) * half * rows), :],
                  cores[a].at[spot(place, step), :], orders[a][chain])
    for a in (0, 1):
        join(a, 0)
        for at, line in enumerate(lines(flip(places[a], chain - 1), near, chain - 1)):
            for unit in range(near, -1, -1):
                forward(a, chain - 1, (at, unit), *units(line, near)[unit])
    for which in range(1, chain - near + 1):
        for a in (0, 1):
            join(a, which)
    for step in range(chain - 1, near - 1, -1):
        count = 2 ** (step - near)
        for at in range(count):
            for unit in range(near, -1, -1):
                for a in (0, 1):
                    where, size = units(lines(places[a], near, step)[at], near)[unit]
                    copies[a][step, at, unit].wait_recv()
                    accs[a][spot(where, size), :] = add(a, step, where, size).astype(jnp.bfloat16)
                    if step > near and at < count // 2:
                        forward(a, step - 1, (at, unit), where, size)
                    elif step == near and unit == near:
                        forward(a, near - 1, (), where, size)
    for step in range(near - 1, -1, -1):
        for a in (0, 1):
            copies[a][step,].wait_recv()
            if step:
                first = flip(places[a], step - 1)
                accs[a][spot(first, step - 1), :] = add(a, step, first, step - 1).astype(jnp.bfloat16)
                forward(a, step - 1, (), first, step - 1)
                accs[a][spot(places[a], step - 1), :] = add(a, step, places[a], step - 1).astype(jnp.bfloat16)
            else:
                outs[a][...] = add(a, 0, places[a], 0).astype(jnp.bfloat16)
    for a in (0, 1):
        for copy in copies[a].values():
            copy.wait_send()


def attend_kernel(inner, blk_spans, slots, tab_k, tab_v, q_in, do_in, k_ref, v_ref,
                  dq_ref, dk_ref, dv_ref, at_k, at_v, ks, vs, q_ref, do_ref, sem, *kept):
    fetches = [pltpu.make_async_copy(q_in, q_ref, sem.at[0]), pltpu.make_async_copy(do_in, do_ref, sem.at[1])]
    for fetch in fetches:
        fetch.start()
    spans = slots.shape[0]
    span = q_ref.shape[0] // 2
    hd = k_ref.shape[1]
    group = q_ref.shape[1] // hd
    blk = blk_spans * span
    scale = 1.0 / math.sqrt(hd)
    f32 = jnp.float32
    linear = lax.axis_index("outer") * inner + lax.axis_index("inner")

    def note(j, _):
        s = slots[j]
        at_k[s] = tab_k[j] * span
        at_v[s] = tab_v[j] * span
        return 0

    lax.fori_loop(0, spans, note, 0)
    tops = [slots[2 * linear], slots[2 * linear + 1]]
    lasts = [top // blk_spans for top in tops]

    def rows_at(table, s):
        return pl.ds(pl.multiple_of(table[s], span), span)

    nt = (((1,), (1,)), ((), ()))
    tn = (((0,), (0,)), ((), ()))
    width = group * span

    def stack(ref):
        return jnp.concatenate(
            [ref[g * span:(g + 1) * span, h * hd:(h + 1) * hd] for g in (0, 1) for h in range(group)], axis=0)

    for fetch in fetches:
        fetch.wait()
    q, do = stack(q_ref), stack(do_ref)
    lane = lax.broadcasted_iota(jnp.int32, (1, 2 * width), 1)
    q_pos = lane % span + jnp.where(lane < width, tops[0], tops[1]) * span
    low = lax.broadcasted_iota(jnp.int32, (blk, 1), 0)

    def logits(k, n, first, masked):
        t = lax.dot_general(k, q[first:], nt, preferred_element_type=f32) * (scale * LOG2E)
        if masked:
            t = jnp.where(low + n * blk <= q_pos[:, first:], t, NEG_FILL)
        return t

    def stats(n, carry, first, masked):
        top, total, weighted = carry
        at = pl.ds(pl.multiple_of(n * blk, blk), blk)
        spots = [(n * blk_spans + j) for j in range(blk_spans)]
        k = jnp.concatenate([k_ref[rows_at(at_k, s), :] for s in spots], axis=0)
        v = jnp.concatenate([v_ref[rows_at(at_v, s), :] for s in spots], axis=0)
        ks[at, :] = k
        vs[at, :] = v
        t = logits(k, n, first, masked)
        dp = lax.dot_general(v, do[first:], nt, preferred_element_type=f32)
        new = jnp.maximum(top, jnp.max(t, axis=0, keepdims=True))
        shrink = jnp.exp2(top - new)
        e = jnp.exp2(t - new)
        if kept:
            kept[0][at, first:] = e
            kept[1][at, first:] = dp
            kept[2][n, :, first:] = new
        return (new, total * shrink + jnp.sum(e, axis=0, keepdims=True),
                weighted * shrink + jnp.sum(e * dp, axis=0, keepdims=True))

    def sweep(step, carry, narrow):
        carry = lax.fori_loop(0, lasts[0], functools.partial(step, first=0, masked=False), carry)
        carry = step(lasts[0], carry, 0, True)
        late = narrow(carry)
        late = lax.fori_loop(lasts[0] + 1, lasts[1], functools.partial(step, first=width, masked=False), late)
        return carry, step(lasts[1], late, width, True)

    start = (jnp.full((1, 2 * width), NEG_FILL, f32), jnp.zeros((1, 2 * width), f32), jnp.zeros((1, 2 * width), f32))
    early, late = sweep(stats, start, lambda carry: tuple(x[:, width:] for x in carry))
    top, total, weighted = [jnp.concatenate([x[:, :width], y], axis=1) for x, y in zip(early, late)]
    lse = top + jnp.log2(total)
    delta = weighted / total

    def grads(n, dq, first, masked):
        at = pl.ds(pl.multiple_of(n * blk, blk), blk)
        k, v = ks[at, :], vs[at, :]
        if kept:
            p = kept[0][at, first:] * jnp.exp2(kept[2][n, :, first:] - lse[:, first:])
            dp = kept[1][at, first:]
        else:
            p = jnp.exp2(logits(k, n, first, masked) - lse[:, first:])
            dp = lax.dot_general(v, do[first:], nt, preferred_element_type=f32)
        ds = (p * (dp - delta[:, first:]) * scale).astype(jnp.bfloat16)
        dk = jnp.dot(ds, q[first:], preferred_element_type=f32).astype(jnp.bfloat16)
        dv = jnp.dot(p.astype(jnp.bfloat16), do[first:], preferred_element_type=f32).astype(jnp.bfloat16)
        for j in range(blk_spans):
            s = n * blk_spans + j
            dk_ref[rows_at(at_k, s), :] = dk[j * span:(j + 1) * span]
            dv_ref[rows_at(at_v, s), :] = dv[j * span:(j + 1) * span]
        return dq + lax.dot_general(k, ds, tn, preferred_element_type=f32)

    early, late = sweep(grads, jnp.zeros((hd, 2 * width), f32), lambda dq: dq[:, width:])
    dq = jnp.concatenate([early[:, :width], late], axis=1).T
    for g in (0, 1):
        for h in range(group):
            at = (g * group + h) * span
            dq_ref[g * span:(g + 1) * span, h * hd:(h + 1) * hd] = dq[at:at + span].astype(jnp.bfloat16)

    def blank(s, _):
        none = jnp.zeros((span, hd), jnp.bfloat16)
        dk_ref[rows_at(at_k, s), :] = none
        dv_ref[rows_at(at_v, s), :] = none
        return 0

    lax.fori_loop((lasts[1] + 1) * blk_spans, spans, blank, 0)


def local(outer, inner, queries, keys, values, grad_out, span_slot):
    rows, hd = keys.shape
    total = rows * outer * inner
    spans = span_slot.shape[0]
    orders = bits_of(outer, inner)
    low = jnp.bfloat16
    vmem, smem = pl.BlockSpec(memory_space=pltpu.VMEM), pl.BlockSpec(memory_space=pltpu.SMEM)
    moves = moves_of(inner.bit_length() - 1, outer.bit_length() - 2)
    hbm = pl.BlockSpec(memory_space=pltpu.HBM)
    sems = [pltpu.SemaphoreType.DMA((2, moves)), pltpu.SemaphoreType.DMA((2, moves))]
    unit = total * hd
    whole = jax.ShapeDtypeStruct((total, hd), low)
    block = jax.ShapeDtypeStruct((rows, hd), low)
    keys_all, values_all = pl.pallas_call(
        functools.partial(gather_kernel, orders),
        out_shape=(whole, whole), in_specs=[hbm] * 2, out_specs=(vmem, vmem),
        scratch_shapes=sems + [pltpu.SemaphoreType.DMA((2,))],
        compiler_params=pltpu.CompilerParams(
            collective_id=0, has_side_effects=True, vmem_limit_bytes=4 * unit + 4 * MIB),
    )(keys, values)
    tables = [
        jnp.asarray(np.array([2 * place_of(order, j // 2 // inner, j // 2 % inner) + j % 2 for j in range(spans)], np.int32))
        for order in orders
    ]
    blk_spans = math.gcd(spans, 4)
    lanes = rows * queries.shape[1] // hd
    kept = []
    if 8 * total * lanes <= 32 * MIB:
        kept = [pltpu.VMEM((total, lanes), jnp.float32), pltpu.VMEM((total, lanes), jnp.float32),
                pltpu.VMEM((spans // blk_spans, 1, lanes), jnp.float32)]
    grad_queries, dk, dv = pl.pallas_call(
        functools.partial(attend_kernel, inner, blk_spans),
        out_shape=(jax.ShapeDtypeStruct(queries.shape, low), whole, whole),
        in_specs=[smem] * 3 + [hbm] * 2 + [vmem] * 2, out_specs=(vmem, vmem, vmem),
        scratch_shapes=[pltpu.SMEM((spans,), jnp.int32), pltpu.SMEM((spans,), jnp.int32),
                        pltpu.VMEM((total, hd), low), pltpu.VMEM((total, hd), low),
                        pltpu.VMEM(queries.shape, low), pltpu.VMEM(queries.shape, low),
                        pltpu.SemaphoreType.DMA((2,))] + kept,
        compiler_params=pltpu.CompilerParams(
            vmem_limit_bytes=12 * unit + 12 * MIB + (9 * total * lanes if kept else 0)),
    )(span_slot, *tables, queries, grad_out, keys_all, values_all)
    grad_keys, grad_values = pl.pallas_call(
        functools.partial(scatter_kernel, orders),
        out_shape=(block, block), in_specs=[vmem] * 2, out_specs=(vmem, vmem),
        scratch_shapes=[pltpu.VMEM((total // 2, hd), low), pltpu.VMEM((total // 2, hd), low),
                        pltpu.VMEM((total // 2, hd), low), pltpu.VMEM((total // 2, hd), low),
                        pltpu.VMEM((total // 2, hd), low), pltpu.VMEM((total // 2, hd), low)] + sems,
        compiler_params=pltpu.CompilerParams(
            collective_id=1, has_side_effects=True, vmem_limit_bytes=10 * unit + 4 * MIB),
    )(dk, dv)
    return grad_queries, grad_keys, grad_values


def solution(mesh):
    rows = P(("outer", "inner"), None)
    return jax.shard_map(
        functools.partial(local, mesh.shape["outer"], mesh.shape["inner"]),
        mesh=mesh,
        in_specs=(rows, rows, rows, rows, P()),
        out_specs=(rows, rows, rows),
        check_vma=False,
    )
```

profile of v0, /device:TPU:0, one launch (start us, length us, event | category | flops | bytes accessed | tf_op | source)
XLA Modules:
  0.0 62.1 jit_solution(10313162166327858261)
XLA Ops:
  0.6 0.0 copy-start.2
  0.6 0.7 %copy-done.2 = bf16[128,128]{1,0:T(8,128)(2,1)S(1)} copy-done((bf16[128,128]{1,0:T(8,128)(2,1)S(1)}, bf16[128,128]{1,0:T(8,128)(2,1)}, u32[]{:S(2)}) %copy-start.2) | copy-done | bytes 32792
  1.4 0.0 copy-start.3
  1.4 0.8 %copy-done.3 = bf16[128,128]{1,0:T(8,128)(2,1)S(1)} copy-done((bf16[128,128]{1,0:T(8,128)(2,1)S(1)}, bf16[128,128]{1,0:T(8,128)(2,1)}, u32[]{:S(2)}) %copy-start.3) | copy-done | bytes 32792
  2.1 21.7 %shard_map.94 = (bf16[4096,128]{1,0:T(8,128)(2,1)S(1)}, bf16[4096,128]{1,0:T(8,128)(2,1)S(1)}) custom-call(bf16[128,128]{1,0:T(8,128)(2,1)S(1)} %copy-done.2, bf16[128,128]{1,0:T(8,128)(2,1)S(1)} %copy-done.3), custom_call_target="tpu_custom_call" | custom-call | tf_op jit(solution)/shard_map/pallas_call | solution.py:353
  23.8 0.0 copy-start.4
  23.8 0.0 copy-start.5
  23.8 0.0 copy-start.6
  23.9 0.6 %copy-done.4 = s32[64]{0:T(128)S(1)} copy-done((s32[64]{0:T(128)S(1)}, s32[64]{0:T(128)}, u32[]{:S(2)}) %copy-start.4) | copy-done | bytes 280
  24.5 0.0 copy-done.5
  24.5 0.0 copy-done.6
  24.5 0.0 copy-start
  24.5 0.9 %copy-done = bf16[128,768]{1,0:T(8,128)(2,1)S(1)} copy-done((bf16[128,768]{1,0:T(8,128)(2,1)S(1)}, bf16[128,768]{1,0:T(8,128)(2,1)}, u32[]{:S(2)}) %copy-start) | copy-done | bytes 196632
  25.4 0.0 copy-start.1
  25.4 0.9 %copy-done.1 = bf16[128,768]{1,0:T(8,128)(2,1)S(1)} copy-done((bf16[128,768]{1,0:T(8,128)(2,1)S(1)}, bf16[128,768]{1,0:T(8,128)(2,1)}, u32[]{:S(2)}) %copy-start.1) | copy-done | bytes 196632
  26.4 11.0 %shard_map.95 = (bf16[128,768]{1,0:T(8,128)(2,1)}, bf16[4096,128]{1,0:T(8,128)(2,1)S(1)}, bf16[4096,128]{1,0:T(8,128)(2,1)S(1)}) custom-call(s32[64]{0:T(128)S(1)} %copy-done.4, s32[64]{0:T(128)S(1)} %copy-done.6, s32[64]{0:T(128)S(1)} %copy-done.5, bf16[128,768]{1,0:T(8,128)(2,1)S(1)} %copy-done, bf16[128,768]{1,0:T(8,128)(2,1)S(1)} %copy-done.1, ...), custom_call_target="tpu_custom_call" | custom-call | tf_op jit(solution)/shard_map/pallas_call | solution.py:370
  37.4 23.5 %shard_map.96 = (bf16[128,128]{1,0:T(8,128)(2,1)S(1)}, bf16[128,128]{1,0:T(8,128)(2,1)S(1)}) custom-call(bf16[4096,128]{1,0:T(8,128)(2,1)S(1)} %get-tuple-element.13.k_in, bf16[4096,128]{1,0:T(8,128)(2,1)S(1)} %get-tuple-element.14.v_in), custom_call_target="tpu_custom_call" | custom-call | tf_op jit(solution)/shard_map/pallas_call | solution.py:381
  60.8 0.6 copy.12
  61.5 0.6 copy.13
Async XLA Ops:
  0.6 0.8 %copy-start.2 = (bf16[128,128]{1,0:T(8,128)(2,1)S(1)}, bf16[128,128]{1,0:T(8,128)(2,1)}, u32[]{:S(2)}) copy-start(bf16[128,128]{1,0:T(8,128)(2,1)} %k_in.1) | copy-start | bytes 98308
  1.4 0.8 %copy-start.3 = (bf16[128,128]{1,0:T(8,128)(2,1)S(1)}, bf16[128,128]{1,0:T(8,128)(2,1)}, u32[]{:S(2)}) copy-start(bf16[128,128]{1,0:T(8,128)(2,1)} %v_in.1) | copy-start | bytes 98308
  23.8 0.7 %copy-start.4 = (s32[64]{0:T(128)S(1)}, s32[64]{0:T(128)}, u32[]{:S(2)}) copy-start(s32[64]{0:T(128)} %slots.1) | copy-start | bytes 772
  23.8 0.7 %copy-start.5 = (s32[64]{0:T(128)S(1)}, s32[64]{0:T(128)}, u32[]{:S(2)}) copy-start(s32[64]{0:T(128)} %constant.5.clone.tab_v) | copy-start | bytes 772
  23.8 0.7 %copy-start.6 = (s32[64]{0:T(128)S(1)}, s32[64]{0:T(128)}, u32[]{:S(2)}) copy-start(s32[64]{0:T(128)} %constant.4.clone.tab_k) | copy-start | bytes 772
  24.5 0.9 %copy-start = (bf16[128,768]{1,0:T(8,128)(2,1)S(1)}, bf16[128,768]{1,0:T(8,128)(2,1)}, u32[]{:S(2)}) copy-start(bf16[128,768]{1,0:T(8,128)(2,1)} %q_in.1) | copy-start | bytes 589828
  25.4 0.9 %copy-start.1 = (bf16[128,768]{1,0:T(8,128)(2,1)S(1)}, bf16[128,768]{1,0:T(8,128)(2,1)}, u32[]{:S(2)}) copy-start(bf16[128,768]{1,0:T(8,128)(2,1)} %do_in.1) | copy-start | bytes 589828
where the time goes:
time: 61.8 us; the launch traced here: 62.1 us
  Pallas kernels  56.1 us (91%)
  local copies, waits for them, and re-layouts  5.26 us (9%)
  between operations  0.69 us (1%)
    pallas_call x1, Pallas kernels, local(): pl.pallas_call(functools.partial(scatter_kernel, orders), out_shape=(bloc...  23.5 us
    pallas_call x1, Pallas kernels, local(): pl.pallas_call(functools.partial(gather_kernel, orders), out_shape=(whole...  21.7 us
    pallas_call x1, Pallas kernels, local(): pl.pallas_call(functools.partial(attend_kernel, inner, blk_spans), out_sh...  11 us
    unnamed x16, local copies, waits for them, and re-layouts  5.26 us

commit v1 on v0

--- a/solution.py
+++ b/solution.py
@@ -57,7 +57,7 @@
 
 
 def moves_of(near, chips):
-    return near + (near + 1) * (2**chips - 1) + chips + 1
+    return near + (near + 1) * (2**chips - 1 + 2 ** (chips - 1)) + chips + 2 ** (chips - 1)
 
 
 def gather_kernel(orders, k_in, v_in, k_out, v_out, send, recv, own):
@@ -122,13 +122,19 @@
                 for a in (0, 1):
                     arrive(a, (path, unit))
                     spread(a, path, unit, path[-1] + 1)
-    for bit in range(near, chain):
+    for bit in range(near, chain - 1):
         for a in (0, 1):
-            for unit in range(near + 1):
-                for path in paths[1:]:
-                    if path[-1] == bit and (a, (path, unit)) not in waited:
-                        arrive(a, (path, unit))
             begin(a, ("core", bit), span_of(flip(places[a], bit), bit), orders[a][chain])
+    for unit in range(near + 1):
+        for path in paths[1:]:
+            if path[-1] == chain - 1:
+                for a in (0, 1):
+                    arrive(a, (path, unit))
+                    place = places[a]
+                    for bit in path:
+                        place = flip(place, bit)
+                    where, size = units(place, near)[unit]
+                    begin(a, ("core", path, unit), span_of(where, size), orders[a][chain])
     for a in (0, 1):
         for name, copy in copies[a].items():
             copy.wait_send()
@@ -173,7 +179,8 @@
         return accs[a][spot(place, size), :].astype(jnp.float32) + got.astype(jnp.float32)
 
     def pieces(a):
-        return [(flip(places[a], step), step) for step in range(chain - 1, near - 1, -1)] + [(places[a], near)]
+        return [(line, near) for line in lines(flip(places[a], chain - 1), near, chain - 1)] + [
+            (flip(places[a], step), step) for step in range(chain - 2, near - 1, -1)] + [(places[a], near)]
 
     def join(a, which):
         place, step = pieces(a)[which]
@@ -182,17 +189,18 @@
         total = mine.astype(jnp.float32) + cores[a][spot(place, step), :].astype(jnp.float32)
         accs[a][spot(place, step), :] = total.astype(jnp.bfloat16)
 
-    for which in range(chain - near + 1):
+    ahead = 2 ** (chain - 1 - near)
+    for which in range(ahead + chain - near):
         for a in (0, 1):
             place, step = pieces(a)[which]
             begin(a, ("core", which), ins[a].at[spot(place, step, (1 - sides[a]) * half * rows), :],
                   cores[a].at[spot(place, step), :], orders[a][chain])
-    for a in (0, 1):
-        join(a, 0)
-        for at, line in enumerate(lines(flip(places[a], chain - 1), near, chain - 1)):
+    for at in range(ahead):
+        for a in (0, 1):
+            join(a, at)
             for unit in range(near, -1, -1):
-                forward(a, chain - 1, (at, unit), *units(line, near)[unit])
-    for which in range(1, chain - near + 1):
+                forward(a, chain - 1, (at, unit), *units(pieces(a)[at][0], near)[unit])
+    for which in range(ahead, ahead + chain - near):
         for a in (0, 1):
             join(a, which)
     for step in range(chain - 1, near - 1, -1):

time: 61.8 us -> 61.4 us (level)
    pallas_call x1, Pallas kernels: 23.5 us -> 22.8 us  [local(): pl.pallas_call(functools.partial(scatter_kernel, orders), out_shape=(bloc...]
where the time goes in v1:
time: 61.4 us; the launch traced here: 61.8 us
  Pallas kernels  55.8 us (91%)
  local copies, waits for them, and re-layouts  5.26 us (9%)
  between operations  0.69 us (1%)
    pallas_call x1, Pallas kernels, local(): pl.pallas_call(functools.partial(scatter_kernel, orders), out_shape=(bloc...  22.8 us
    pallas_call x1, Pallas kernels, local(): pl.pallas_call(functools.partial(gather_kernel, orders), out_shape=(whole...  21.6 us
    pallas_call x1, Pallas kernels, local(): pl.pallas_call(functools.partial(attend_kernel, inner, blk_spans), out_sh...  11.3 us
    unnamed x16, local copies, waits for them, and re-layouts  5.26 us

profile of v1, /device:TPU:0, one launch (start us, length us, event | category | flops | bytes accessed | tf_op | source)
XLA Modules:
  0.0 61.8 jit_solution(2713174951706730344)
XLA Ops:
  0.6 0.0 copy-start.2
  0.6 0.7 %copy-done.2 = bf16[128,128]{1,0:T(8,128)(2,1)S(1)} copy-done((bf16[128,128]{1,0:T(8,128)(2,1)S(1)}, bf16[128,128]{1,0:T(8,128)(2,1)}, u32[]{:S(2)}) %copy-start.2) | copy-done | bytes 32792
  1.4 0.0 copy-start.3
  1.4 0.8 %copy-done.3 = bf16[128,128]{1,0:T(8,128)(2,1)S(1)} copy-done((bf16[128,128]{1,0:T(8,128)(2,1)S(1)}, bf16[128,128]{1,0:T(8,128)(2,1)}, u32[]{:S(2)}) %copy-start.3) | copy-done | bytes 32792
  2.1 21.6 %shard_map.94 = (bf16[4096,128]{1,0:T(8,128)(2,1)S(1)}, bf16[4096,128]{1,0:T(8,128)(2,1)S(1)}) custom-call(bf16[128,128]{1,0:T(8,128)(2,1)S(1)} %copy-done.2, bf16[128,128]{1,0:T(8,128)(2,1)S(1)} %copy-done.3), custom_call_target="tpu_custom_call" | custom-call | tf_op jit(solution)/shard_map/pallas_call | solution.py:361
  23.8 0.0 copy-start.4
  23.8 0.0 copy-start.5
  23.8 0.0 copy-start.6
  23.8 0.6 %copy-done.4 = s32[64]{0:T(128)S(1)} copy-done((s32[64]{0:T(128)S(1)}, s32[64]{0:T(128)}, u32[]{:S(2)}) %copy-start.4) | copy-done | bytes 280
  24.5 0.0 copy-done.5
  24.5 0.0 copy-done.6
  24.5 0.0 copy-start
  24.5 0.9 %copy-done = bf16[128,768]{1,0:T(8,128)(2,1)S(1)} copy-done((bf16[128,768]{1,0:T(8,128)(2,1)S(1)}, bf16[128,768]{1,0:T(8,128)(2,1)}, u32[]{:S(2)}) %copy-start) | copy-done | bytes 196632
  25.4 0.0 copy-start.1
  25.4 0.9 %copy-done.1 = bf16[128,768]{1,0:T(8,128)(2,1)S(1)} copy-done((bf16[128,768]{1,0:T(8,128)(2,1)S(1)}, bf16[128,768]{1,0:T(8,128)(2,1)}, u32[]{:S(2)}) %copy-start.1) | copy-done | bytes 196632
  26.4 11.3 %shard_map.95 = (bf16[128,768]{1,0:T(8,128)(2,1)}, bf16[4096,128]{1,0:T(8,128)(2,1)S(1)}, bf16[4096,128]{1,0:T(8,128)(2,1)S(1)}) custom-call(s32[64]{0:T(128)S(1)} %copy-done.4, s32[64]{0:T(128)S(1)} %copy-done.6, s32[64]{0:T(128)S(1)} %copy-done.5, bf16[128,768]{1,0:T(8,128)(2,1)S(1)} %copy-done, bf16[128,768]{1,0:T(8,128)(2,1)S(1)} %copy-done.1, ...), custom_call_target="tpu_custom_call" | custom-call | tf_op jit(solution)/shard_map/pallas_call | solution.py:378
  37.7 22.8 %shard_map.96 = (bf16[128,128]{1,0:T(8,128)(2,1)S(1)}, bf16[128,128]{1,0:T(8,128)(2,1)S(1)}) custom-call(bf16[4096,128]{1,0:T(8,128)(2,1)S(1)} %get-tuple-element.13.k_in, bf16[4096,128]{1,0:T(8,128)(2,1)S(1)} %get-tuple-element.14.v_in), custom_call_target="tpu_custom_call" | custom-call | tf_op jit(solution)/shard_map/pallas_call | solution.py:389
  60.5 0.6 copy.12
  61.2 0.6 copy.13
Async XLA Ops:
  0.6 0.8 %copy-start.2 = (bf16[128,128]{1,0:T(8,128)(2,1)S(1)}, bf16[128,128]{1,0:T(8,128)(2,1)}, u32[]{:S(2)}) copy-start(bf16[128,128]{1,0:T(8,128)(2,1)} %k_in.1) | copy-start | bytes 98308
  1.4 0.8 %copy-start.3 = (bf16[128,128]{1,0:T(8,128)(2,1)S(1)}, bf16[128,128]{1,0:T(8,128)(2,1)}, u32[]{:S(2)}) copy-start(bf16[128,128]{1,0:T(8,128)(2,1)} %v_in.1) | copy-start | bytes 98308
  23.8 0.7 %copy-start.4 = (s32[64]{0:T(128)S(1)}, s32[64]{0:T(128)}, u32[]{:S(2)}) copy-start(s32[64]{0:T(128)} %slots.1) | copy-start | bytes 772
  23.8 0.7 %copy-start.5 = (s32[64]{0:T(128)S(1)}, s32[64]{0:T(128)}, u32[]{:S(2)}) copy-start(s32[64]{0:T(128)} %constant.5.clone.tab_v) | copy-start | bytes 772
  23.8 0.7 %copy-start.6 = (s32[64]{0:T(128)S(1)}, s32[64]{0:T(128)}, u32[]{:S(2)}) copy-start(s32[64]{0:T(128)} %constant.4.clone.tab_k) | copy-start | bytes 772
  24.5 0.9 %copy-start = (bf16[128,768]{1,0:T(8,128)(2,1)S(1)}, bf16[128,768]{1,0:T(8,128)(2,1)}, u32[]{:S(2)}) copy-start(bf16[128,768]{1,0:T(8,128)(2,1)} %q_in.1) | copy-start | bytes 589828
  25.4 0.9 %copy-start.1 = (bf16[128,768]{1,0:T(8,128)(2,1)S(1)}, bf16[128,768]{1,0:T(8,128)(2,1)}, u32[]{:S(2)}) copy-start(bf16[128,768]{1,0:T(8,128)(2,1)} %do_in.1) | copy-start | bytes 589828

commit v2 on v1

--- a/solution.py
+++ b/solution.py
@@ -230,11 +230,8 @@
             copy.wait_send()
 
 
-def attend_kernel(inner, blk_spans, slots, tab_k, tab_v, q_in, do_in, k_ref, v_ref,
-                  dq_ref, dk_ref, dv_ref, at_k, at_v, ks, vs, q_ref, do_ref, sem, *kept):
-    fetches = [pltpu.make_async_copy(q_in, q_ref, sem.at[0]), pltpu.make_async_copy(do_in, do_ref, sem.at[1])]
-    for fetch in fetches:
-        fetch.start()
+def attend_kernel(inner, blk_spans, slots, tab_k, tab_v, q_ref, do_ref, k_ref, v_ref,
+                  dq_ref, dk_ref, dv_ref, at_k, at_v, ks, vs, *kept):
     spans = slots.shape[0]
     span = q_ref.shape[0] // 2
     hd = k_ref.shape[1]
@@ -265,8 +262,6 @@
         return jnp.concatenate(
             [ref[g * span:(g + 1) * span, h * hd:(h + 1) * hd] for g in (0, 1) for h in range(group)], axis=0)
 
-    for fetch in fetches:
-        fetch.wait()
     q, do = stack(q_ref), stack(do_ref)
     lane = lax.broadcasted_iota(jnp.int32, (1, 2 * width), 1)
     q_pos = lane % span + jnp.where(lane < width, tops[0], tops[1]) * span
@@ -278,10 +273,10 @@
             t = jnp.where(low + n * blk <= q_pos[:, first:], t, NEG_FILL)
         return t
 
-    def stats(n, carry, first, masked):
+    def stats(n, carry, first, masked, blocks=1):
         top, total, weighted = carry
-        at = pl.ds(pl.multiple_of(n * blk, blk), blk)
-        spots = [(n * blk_spans + j) for j in range(blk_spans)]
+        at = pl.ds(pl.multiple_of(n * blk, blk), blocks * blk)
+        spots = [(n * blk_spans + j) for j in range(blocks * blk_spans)]
         k = jnp.concatenate([k_ref[rows_at(at_k, s), :] for s in spots], axis=0)
         v = jnp.concatenate([v_ref[rows_at(at_v, s), :] for s in spots], axis=0)
         ks[at, :] = k
@@ -298,11 +293,16 @@
         return (new, total * shrink + jnp.sum(e, axis=0, keepdims=True),
                 weighted * shrink + jnp.sum(e * dp, axis=0, keepdims=True))
 
+    def run(step, begin, end, first, carry):
+        pairs = (end - begin) // 2
+        carry = lax.fori_loop(
+            0, pairs, lambda n, c: step(begin + 2 * n, c, first, False, 2), carry)
+        return lax.fori_loop(begin + 2 * pairs, end, lambda n, c: step(n, c, first, False), carry)
+
     def sweep(step, carry, narrow):
-        carry = lax.fori_loop(0, lasts[0], functools.partial(step, first=0, masked=False), carry)
+        carry = run(step, 0, lasts[0], 0, carry)
         carry = step(lasts[0], carry, 0, True)
-        late = narrow(carry)
-        late = lax.fori_loop(lasts[0] + 1, lasts[1], functools.partial(step, first=width, masked=False), late)
+        late = run(step, lasts[0] + 1, lasts[1], width, narrow(carry))
         return carry, step(lasts[1], late, width, True)
 
     start = (jnp.full((1, 2 * width), NEG_FILL, f32), jnp.zeros((1, 2 * width), f32), jnp.zeros((1, 2 * width), f32))
@@ -311,8 +311,8 @@
     lse = top + jnp.log2(total)
     delta = weighted / total
 
-    def grads(n, dq, first, masked):
-        at = pl.ds(pl.multiple_of(n * blk, blk), blk)
+    def grads(n, dq, first, masked, blocks=1):
+        at = pl.ds(pl.multiple_of(n * blk, blk), blocks * blk)
         k, v = ks[at, :], vs[at, :]
         if kept:
             p = kept[0][at, first:] * jnp.exp2(kept[2][n, :, first:] - lse[:, first:])
@@ -323,7 +323,7 @@
         ds = (p * (dp - delta[:, first:]) * scale).astype(jnp.bfloat16)
         dk = jnp.dot(ds, q[first:], preferred_element_type=f32).astype(jnp.bfloat16)
         dv = jnp.dot(p.astype(jnp.bfloat16), do[first:], preferred_element_type=f32).astype(jnp.bfloat16)
-        for j in range(blk_spans):
+        for j in range(blocks * blk_spans):
             s = n * blk_spans + j
             dk_ref[rows_at(at_k, s), :] = dk[j * span:(j + 1) * span]
             dv_ref[rows_at(at_v, s), :] = dv[j * span:(j + 1) * span]
@@ -364,6 +364,7 @@
         scratch_shapes=sems + [pltpu.SemaphoreType.DMA((2,))],
         compiler_params=pltpu.CompilerParams(
             collective_id=0, has_side_effects=True, vmem_limit_bytes=4 * unit + 4 * MIB),
+        cost_estimate=pl.CostEstimate(flops=0, bytes_accessed=64 * unit, transcendentals=0),
     )(keys, values)
     tables = [
         jnp.asarray(np.array([2 * place_of(order, j // 2 // inner, j // 2 % inner) + j % 2 for j in range(spans)], np.int32))
@@ -378,11 +379,9 @@
     grad_queries, dk, dv = pl.pallas_call(
         functools.partial(attend_kernel, inner, blk_spans),
         out_shape=(jax.ShapeDtypeStruct(queries.shape, low), whole, whole),
-        in_specs=[smem] * 3 + [hbm] * 2 + [vmem] * 2, out_specs=(vmem, vmem, vmem),
+        in_specs=[smem] * 3 + [vmem] * 4, out_specs=(vmem, vmem, vmem),
         scratch_shapes=[pltpu.SMEM((spans,), jnp.int32), pltpu.SMEM((spans,), jnp.int32),
-                        pltpu.VMEM((total, hd), low), pltpu.VMEM((total, hd), low),
-                        pltpu.VMEM(queries.shape, low), pltpu.VMEM(queries.shape, low),
-                        pltpu.SemaphoreType.DMA((2,))] + kept,
+                        pltpu.VMEM((total, hd), low), pltpu.VMEM((total, hd), low)] + kept,
         compiler_params=pltpu.CompilerParams(
             vmem_limit_bytes=12 * unit + 12 * MIB + (9 * total * lanes if kept else 0)),
     )(span_slot, *tables, queries, grad_out, keys_all, values_all)

time: 61.4 us -> 58.4 us (0.951); the launches traced: 61.8 us -> 57.7 us
  Pallas kernels: 55.8 us -> 51.8 us
    pallas_call x1, Pallas kernels: 11.3 us -> 9.06 us  [local(): pl.pallas_call(functools.partial(attend_kernel, inner, blk_spans), out_sh...]
    pallas_call x1, Pallas kernels: 22.8 us -> 21.1 us  [local(): pl.pallas_call(functools.partial(scatter_kernel, orders), out_shape=(bloc...]
where the time goes in v2:
time: 58.4 us; the launch traced here: 57.7 us
  Pallas kernels  51.8 us (89%)
  local copies, waits for them, and re-layouts  5.26 us (9%)
  between operations  0.68 us (1%)
    pallas_call x1, Pallas kernels, local(): pl.pallas_call(functools.partial(gather_kernel, orders), out_shape=(whole...  21.6 us
    pallas_call x1, Pallas kernels, local(): pl.pallas_call(functools.partial(scatter_kernel, orders), out_shape=(bloc...  21.1 us
    pallas_call x1, Pallas kernels, local(): pl.pallas_call(functools.partial(attend_kernel, inner, blk_spans), out_sh...  9.06 us
    unnamed x16, local copies, waits for them, and re-layouts  5.26 us

profile of v2, /device:TPU:0, one launch (start us, length us, event | category | flops | bytes accessed | tf_op | source)
XLA Modules:
  0.0 57.7 jit_solution(6421248283188170428)
XLA Ops:
  0.6 0.0 copy-start.2
  0.6 0.7 %copy-done.2 = bf16[128,128]{1,0:T(8,128)(2,1)S(1)} copy-done((bf16[128,128]{1,0:T(8,128)(2,1)S(1)}, bf16[128,128]{1,0:T(8,128)(2,1)}, u32[]{:S(2)}) %copy-start.2) | copy-done | bytes 32792
  1.4 0.0 copy-start.3
  1.4 0.8 %copy-done.3 = bf16[128,128]{1,0:T(8,128)(2,1)S(1)} copy-done((bf16[128,128]{1,0:T(8,128)(2,1)S(1)}, bf16[128,128]{1,0:T(8,128)(2,1)}, u32[]{:S(2)}) %copy-start.3) | copy-done | bytes 32792
  2.1 21.6 %shard_map.94 = (bf16[4096,128]{1,0:T(8,128)(2,1)S(1)}, bf16[4096,128]{1,0:T(8,128)(2,1)S(1)}) custom-call(bf16[128,128]{1,0:T(8,128)(2,1)S(1)} %copy-done.2, bf16[128,128]{1,0:T(8,128)(2,1)S(1)} %copy-done.3), custom_call_target="tpu_custom_call" | custom-call | bytes 33554432 | tf_op jit(solution)/shard_map/pallas_call | solution.py:361
  23.8 0.0 copy-start.4
  23.8 0.0 copy-start.5
  23.8 0.0 copy-start.6
  23.8 0.6 %copy-done.4 = s32[64]{0:T(128)S(1)} copy-done((s32[64]{0:T(128)S(1)}, s32[64]{0:T(128)}, u32[]{:S(2)}) %copy-start.4) | copy-done | bytes 280
  24.5 0.0 copy-done.5
  24.5 0.0 copy-done.6
  24.5 0.0 copy-start
  24.5 0.9 %copy-done = bf16[128,768]{1,0:T(8,128)(2,1)S(1)} copy-done((bf16[128,768]{1,0:T(8,128)(2,1)S(1)}, bf16[128,768]{1,0:T(8,128)(2,1)}, u32[]{:S(2)}) %copy-start) | copy-done | bytes 196632
  25.4 0.0 copy-start.1
  25.4 0.9 %copy-done.1 = bf16[128,768]{1,0:T(8,128)(2,1)S(1)} copy-done((bf16[128,768]{1,0:T(8,128)(2,1)S(1)}, bf16[128,768]{1,0:T(8,128)(2,1)}, u32[]{:S(2)}) %copy-start.1) | copy-done | bytes 196632
  26.4 9.1 %shard_map.95 = (bf16[128,768]{1,0:T(8,128)(2,1)}, bf16[4096,128]{1,0:T(8,128)(2,1)S(1)}, bf16[4096,128]{1,0:T(8,128)(2,1)S(1)}) custom-call(s32[64]{0:T(128)S(1)} %copy-done.4, s32[64]{0:T(128)S(1)} %copy-done.6, s32[64]{0:T(128)S(1)} %copy-done.5, bf16[128,768]{1,0:T(8,128)(2,1)S(1)} %copy-done, bf16[128,768]{1,0:T(8,128)(2,1)S(1)} %copy-done.1, ...), custom_call_target="tpu_custom_call" | custom-call | tf_op jit(solution)/shard_map/pallas_call | solution.py:379
  35.4 21.1 %shard_map.96 = (bf16[128,128]{1,0:T(8,128)(2,1)S(1)}, bf16[128,128]{1,0:T(8,128)(2,1)S(1)}) custom-call(bf16[4096,128]{1,0:T(8,128)(2,1)S(1)} %get-tuple-element.13.k_in, bf16[4096,128]{1,0:T(8,128)(2,1)S(1)} %get-tuple-element.14.v_in), custom_call_target="tpu_custom_call" | custom-call | tf_op jit(solution)/shard_map/pallas_call | solution.py:388
  56.5 0.6 %copy.12 = bf16[128,128]{1,0:T(8,128)(2,1)} copy(bf16[128,128]{1,0:T(8,128)(2,1)S(1)} %get-tuple-element.21) | data formatting | bytes 65536
  57.1 0.6 %copy.13 = bf16[128,128]{1,0:T(8,128)(2,1)} copy(bf16[128,128]{1,0:T(8,128)(2,1)S(1)} %get-tuple-element.22) | data formatting | bytes 65536
Async XLA Ops:
  0.6 0.8 %copy-start.2 = (bf16[128,128]{1,0:T(8,128)(2,1)S(1)}, bf16[128,128]{1,0:T(8,128)(2,1)}, u32[]{:S(2)}) copy-start(bf16[128,128]{1,0:T(8,128)(2,1)} %k_in.1) | copy-start | bytes 98308
  1.4 0.8 %copy-start.3 = (bf16[128,128]{1,0:T(8,128)(2,1)S(1)}, bf16[128,128]{1,0:T(8,128)(2,1)}, u32[]{:S(2)}) copy-start(bf16[128,128]{1,0:T(8,128)(2,1)} %v_in.1) | copy-start | bytes 98308
  23.8 0.7 %copy-start.4 = (s32[64]{0:T(128)S(1)}, s32[64]{0:T(128)}, u32[]{:S(2)}) copy-start(s32[64]{0:T(128)} %slots.1) | copy-start | bytes 772
  23.8 0.7 %copy-start.5 = (s32[64]{0:T(128)S(1)}, s32[64]{0:T(128)}, u32[]{:S(2)}) copy-start(s32[64]{0:T(128)} %constant.5.clone.tab_v) | copy-start | bytes 772
  23.8 0.7 %copy-start.6 = (s32[64]{0:T(128)S(1)}, s32[64]{0:T(128)}, u32[]{:S(2)}) copy-start(s32[64]{0:T(128)} %constant.4.clone.tab_k) | copy-start | bytes 772
  24.5 0.9 %copy-start = (bf16[128,768]{1,0:T(8,128)(2,1)S(1)}, bf16[128,768]{1,0:T(8,128)(2,1)}, u32[]{:S(2)}) copy-start(bf16[128,768]{1,0:T(8,128)(2,1)} %q_ref.1) | copy-start | bytes 589828
  25.4 0.9 %copy-start.1 = (bf16[128,768]{1,0:T(8,128)(2,1)S(1)}, bf16[128,768]{1,0:T(8,128)(2,1)}, u32[]{:S(2)}) copy-start(bf16[128,768]{1,0:T(8,128)(2,1)} %do_ref.1) | copy-start | bytes 589828

commit v3 on v2

--- a/solution.py
+++ b/solution.py
@@ -60,7 +60,7 @@
     return near + (near + 1) * (2**chips - 1 + 2 ** (chips - 1)) + chips + 2 ** (chips - 1)
 
 
-def gather_kernel(orders, k_in, v_in, k_out, v_out, send, recv, own):
+def gather_kernel(orders, k_in, v_in, q_in, do_in, k_out, v_out, q_out, do_out, send, recv, own):
     o, i = lax.axis_index("outer"), lax.axis_index("inner")
     rows = k_in.shape[0]
     chain = len(orders[0]) - 1
@@ -75,7 +75,8 @@
     owned = [
         pltpu.make_async_copy((k_in, v_in)[a], outs[a].at[span_of(places[a], 0), :], own.at[a]) for a in (0, 1)
     ]
-    for copy in owned:
+    fetches = [pltpu.make_async_copy(q_in, q_out, own.at[2]), pltpu.make_async_copy(do_in, do_out, own.at[3])]
+    for copy in owned + fetches:
         copy.start()
     greet(orders[0], o, i)
     copies, waited = ({}, {}), set()
@@ -140,6 +141,8 @@
             copy.wait_send()
             if (a, name) not in waited:
                 copy.wait_recv()
+    for fetch in fetches:
+        fetch.wait()
 
 
 def scatter_kernel(orders, k_in, v_in, k_out, v_out, k_acc, v_acc, k_got, v_got, k_core, v_core, send, recv):
@@ -230,8 +233,12 @@
             copy.wait_send()
 
 
-def attend_kernel(inner, blk_spans, slots, tab_k, tab_v, q_ref, do_ref, k_ref, v_ref,
-                  dq_ref, dk_ref, dv_ref, at_k, at_v, ks, vs, *kept):
+def attend_kernel(inner, blk_spans, slots_in, tab_k_in, tab_v_in, q_ref, do_ref, k_ref, v_ref,
+                  dq_ref, dk_ref, dv_ref, at_k, at_v, slots, tab_k, tab_v, sem, ks, vs, *kept):
+    reads = [pltpu.make_async_copy(src, dst, sem.at[j])
+             for j, (src, dst) in enumerate(((slots_in, slots), (tab_k_in, tab_k), (tab_v_in, tab_v)))]
+    for read in reads:
+        read.start()
     spans = slots.shape[0]
     span = q_ref.shape[0] // 2
     hd = k_ref.shape[1]
@@ -247,6 +254,8 @@
         at_v[s] = tab_v[j] * span
         return 0
 
+    for read in reads:
+        read.wait()
     lax.fori_loop(0, spans, note, 0)
     tops = [slots[2 * linear], slots[2 * linear + 1]]
     lasts = [top // blk_spans for top in tops]
@@ -351,25 +360,28 @@
     spans = span_slot.shape[0]
     orders = bits_of(outer, inner)
     low = jnp.bfloat16
-    vmem, smem = pl.BlockSpec(memory_space=pltpu.VMEM), pl.BlockSpec(memory_space=pltpu.SMEM)
+    vmem = pl.BlockSpec(memory_space=pltpu.VMEM)
     moves = moves_of(inner.bit_length() - 1, outer.bit_length() - 2)
     hbm = pl.BlockSpec(memory_space=pltpu.HBM)
     sems = [pltpu.SemaphoreType.DMA((2, moves)), pltpu.SemaphoreType.DMA((2, moves))]
     unit = total * hd
     whole = jax.ShapeDtypeStruct((total, hd), low)
     block = jax.ShapeDtypeStruct((rows, hd), low)
-    keys_all, values_all = pl.pallas_call(
-        functools.partial(gather_kernel, orders),
-        out_shape=(whole, whole), in_specs=[hbm] * 2, out_specs=(vmem, vmem),
-        scratch_shapes=sems + [pltpu.SemaphoreType.DMA((2,))],
-        compiler_params=pltpu.CompilerParams(
-            collective_id=0, has_side_effects=True, vmem_limit_bytes=4 * unit + 4 * MIB),
-        cost_estimate=pl.CostEstimate(flops=0, bytes_accessed=64 * unit, transcendentals=0),
-    )(keys, values)
     tables = [
         jnp.asarray(np.array([2 * place_of(order, j // 2 // inner, j // 2 % inner) + j % 2 for j in range(spans)], np.int32))
         for order in orders
     ]
+    keys, values, queries, grad_out, *small = (
+        pltpu.with_memory_space_constraint(x, pltpu.HBM)
+        for x in (keys, values, queries, grad_out, span_slot, *tables))
+    keys_all, values_all, queries, grad_out = pl.pallas_call(
+        functools.partial(gather_kernel, orders),
+        out_shape=(whole, whole) + (jax.ShapeDtypeStruct(queries.shape, low),) * 2, in_specs=[hbm] * 4, out_specs=(vmem,) * 4,
+        scratch_shapes=sems + [pltpu.SemaphoreType.DMA((4,))],
+        compiler_params=pltpu.CompilerParams(
+            collective_id=0, has_side_effects=True, vmem_limit_bytes=4 * unit + 4 * MIB),
+        cost_estimate=pl.CostEstimate(flops=0, bytes_accessed=64 * unit, transcendentals=0),
+    )(keys, values, queries, grad_out)
     blk_spans = math.gcd(spans, 4)
     lanes = rows * queries.shape[1] // hd
     kept = []
@@ -379,12 +391,12 @@
     grad_queries, dk, dv = pl.pallas_call(
         functools.partial(attend_kernel, inner, blk_spans),
         out_shape=(jax.ShapeDtypeStruct(queries.shape, low), whole, whole),
-        in_specs=[smem] * 3 + [vmem] * 4, out_specs=(vmem, vmem, vmem),
-        scratch_shapes=[pltpu.SMEM((spans,), jnp.int32), pltpu.SMEM((spans,), jnp.int32),
+        in_specs=[hbm] * 3 + [vmem] * 4, out_specs=(vmem, vmem, vmem),
+        scratch_shapes=[pltpu.SMEM((spans,), jnp.int32)] * 5 + [pltpu.SemaphoreType.DMA((3,)),
                         pltpu.VMEM((total, hd), low), pltpu.VMEM((total, hd), low)] + kept,
         compiler_params=pltpu.CompilerParams(
             vmem_limit_bytes=12 * unit + 12 * MIB + (9 * total * lanes if kept else 0)),
-    )(span_slot, *tables, queries, grad_out, keys_all, values_all)
+    )(*small, queries, grad_out, keys_all, values_all)
     grad_keys, grad_values = pl.pallas_call(
         functools.partial(scatter_kernel, orders),
         out_shape=(block, block), in_specs=[vmem] * 2, out_specs=(vmem, vmem),

time: 58.4 us -> 54.2 us (0.928); the launches traced: 57.7 us -> 54.2 us
  local copies, waits for them, and re-layouts: 5.26 us -> 1.23 us
  Pallas kernels: 51.8 us -> 52.4 us
    unnamed x16 -> x2, local copies, waits for them, and re-layouts: 5.26 us -> 1.23 us
where the time goes in v3:
time: 54.2 us
  Pallas kernels  52.4 us (97%)
  local copies, waits for them, and re-layouts  1.23 us (2%)
  between operations  0.66 us (1%)
    pallas_call x1, Pallas kernels, local(): pl.pallas_call(functools.partial(gather_kernel, orders), out_shape=(whole...  21.7 us
    pallas_call x1, Pallas kernels, local(): pl.pallas_call(functools.partial(scatter_kernel, orders), out_shape=(bloc...  21.2 us
    pallas_call x1, Pallas kernels, local(): pl.pallas_call(functools.partial(attend_kernel, inner, blk_spans), out_sh...  9.51 us
    unnamed x2, local copies, waits for them, and re-layouts  1.23 us

profile of v3, /device:TPU:0, one launch (start us, length us, event | category | flops | bytes accessed | tf_op | source)
XLA Modules:
  0.0 54.2 jit_solution(17745605001076983242)
XLA Ops:
  0.6 21.7 %shard_map.94 = (bf16[4096,128]{1,0:T(8,128)(2,1)S(1)}, bf16[4096,128]{1,0:T(8,128)(2,1)S(1)}, bf16[128,768]{1,0:T(8,128)(2,1)S(1)}, bf16[128,768]{1,0:T(8,128)(2,1)S(1)}) custom-call(bf16[128,128]{1,0:T(8,128)(2,1)} %k_in.1, bf16[128,128]{1,0:T(8,128)(2,1)} %v_in.1, bf16[128,768]{1,0:T(8,128)(2,1)} %q_in.1, bf16[128,768]{1,0:T(8,128)(2,1)} %do_in.1), custom_call_target="tpu_custom_call" | custom-call | bytes 33554432 | tf_op jit(solution)/shard_map/pallas_call | solution.py:377
  22.3 9.5 %shard_map.95 = (bf16[128,768]{1,0:T(8,128)(2,1)}, bf16[4096,128]{1,0:T(8,128)(2,1)S(1)}, bf16[4096,128]{1,0:T(8,128)(2,1)S(1)}) custom-call(s32[64]{0:T(128)} %slots_in.1, s32[64]{0:T(128)} %constant.4.clone.tab_k_in, s32[64]{0:T(128)} %constant.5.clone.tab_v_in, bf16[128,768]{1,0:T(8,128)(2,1)S(1)} %get-tuple-element.12.q_ref, ...), custom_call_target="tpu_custom_call" | custom-call | tf_op jit(solution)/shard_map/pallas_call | solution.py:391
  31.8 21.2 %shard_map.96 = (bf16[128,128]{1,0:T(8,128)(2,1)S(1)}, bf16[128,128]{1,0:T(8,128)(2,1)S(1)}) custom-call(bf16[4096,128]{1,0:T(8,128)(2,1)S(1)} %get-tuple-element.17.k_in, bf16[4096,128]{1,0:T(8,128)(2,1)S(1)} %get-tuple-element.18.v_in), custom_call_target="tpu_custom_call" | custom-call | tf_op jit(solution)/shard_map/pallas_call | solution.py:400
  53.0 0.6 %copy.12 = bf16[128,128]{1,0:T(8,128)(2,1)} copy(bf16[128,128]{1,0:T(8,128)(2,1)S(1)} %get-tuple-element.25) | data formatting | bytes 65536
  53.6 0.6 %copy.13 = bf16[128,128]{1,0:T(8,128)(2,1)} copy(bf16[128,128]{1,0:T(8,128)(2,1)S(1)} %get-tuple-element.26) | data formatting | bytes 65536

commit v4 on v3

--- a/solution.py
+++ b/solution.py
@@ -256,7 +256,7 @@
 
     for read in reads:
         read.wait()
-    lax.fori_loop(0, spans, note, 0)
+    lax.fori_loop(0, spans, note, 0, unroll=8)
     tops = [slots[2 * linear], slots[2 * linear + 1]]
     lasts = [top // blk_spans for top in tops]
 
@@ -303,10 +303,12 @@
                 weighted * shrink + jnp.sum(e * dp, axis=0, keepdims=True))
 
     def run(step, begin, end, first, carry):
-        pairs = (end - begin) // 2
-        carry = lax.fori_loop(
-            0, pairs, lambda n, c: step(begin + 2 * n, c, first, False, 2), carry)
-        return lax.fori_loop(begin + 2 * pairs, end, lambda n, c: step(n, c, first, False), carry)
+        for blocks in (4, 2, 1) if first else (2, 1):
+            count = (end - begin) // blocks
+            carry = lax.fori_loop(
+                0, count, lambda n, c, at=begin, blocks=blocks: step(at + blocks * n, c, first, False, blocks), carry)
+            begin = begin + blocks * count
+        return carry
 
     def sweep(step, carry, narrow):
         carry = run(step, 0, lasts[0], 0, carry)

time: 54.2 us -> 53.7 us (level)
    pallas_call x1, Pallas kernels: 9.51 us -> 8.73 us  [local(): pl.pallas_call(functools.partial(attend_kernel, inner, blk_spans), out_sh...]
where the time goes in v4:
time: 53.7 us; the launch traced here: 53.8 us
  Pallas kernels  51.9 us (97%)
  local copies, waits for them, and re-layouts  1.23 us (2%)
  between operations  0.66 us (1%)
    pallas_call x1, Pallas kernels, local(): pl.pallas_call(functools.partial(gather_kernel, orders), out_shape=(whole...  21.7 us
    pallas_call x1, Pallas kernels, local(): pl.pallas_call(functools.partial(scatter_kernel, orders), out_shape=(bloc...  21.5 us
    pallas_call x1, Pallas kernels, local(): pl.pallas_call(functools.partial(attend_kernel, inner, blk_spans), out_sh...  8.73 us
    unnamed x2, local copies, waits for them, and re-layouts  1.23 us

profile of v4, /device:TPU:0, one launch (start us, length us, event | category | flops | bytes accessed | tf_op | source)
XLA Modules:
  0.0 53.8 jit_solution(12712701728010622718)
XLA Ops:
  0.6 21.7 %shard_map.94 = (bf16[4096,128]{1,0:T(8,128)(2,1)S(1)}, bf16[4096,128]{1,0:T(8,128)(2,1)S(1)}, bf16[128,768]{1,0:T(8,128)(2,1)S(1)}, bf16[128,768]{1,0:T(8,128)(2,1)S(1)}) custom-call(bf16[128,128]{1,0:T(8,128)(2,1)} %k_in.1, bf16[128,128]{1,0:T(8,128)(2,1)} %v_in.1, bf16[128,768]{1,0:T(8,128)(2,1)} %q_in.1, bf16[128,768]{1,0:T(8,128)(2,1)} %do_in.1), custom_call_target="tpu_custom_call" | custom-call | bytes 33554432 | tf_op jit(solution)/shard_map/pallas_call | solution.py:379
  22.3 8.7 %shard_map.95 = (bf16[128,768]{1,0:T(8,128)(2,1)}, bf16[4096,128]{1,0:T(8,128)(2,1)S(1)}, bf16[4096,128]{1,0:T(8,128)(2,1)S(1)}) custom-call(s32[64]{0:T(128)} %slots_in.1, s32[64]{0:T(128)} %constant.4.clone.tab_k_in, s32[64]{0:T(128)} %constant.5.clone.tab_v_in, bf16[128,768]{1,0:T(8,128)(2,1)S(1)} %get-tuple-element.12.q_ref, ...), custom_call_target="tpu_custom_call" | custom-call | tf_op jit(solution)/shard_map/pallas_call | solution.py:393
  31.1 21.5 %shard_map.96 = (bf16[128,128]{1,0:T(8,128)(2,1)S(1)}, bf16[128,128]{1,0:T(8,128)(2,1)S(1)}) custom-call(bf16[4096,128]{1,0:T(8,128)(2,1)S(1)} %get-tuple-element.17.k_in, bf16[4096,128]{1,0:T(8,128)(2,1)S(1)} %get-tuple-element.18.v_in), custom_call_target="tpu_custom_call" | custom-call | tf_op jit(solution)/shard_map/pallas_call | solution.py:402
  52.5 0.6 %copy.12 = bf16[128,128]{1,0:T(8,128)(2,1)} copy(bf16[128,128]{1,0:T(8,128)(2,1)S(1)} %get-tuple-element.25) | data formatting | bytes 65536
  53.2 0.6 %copy.13 = bf16[128,128]{1,0:T(8,128)(2,1)} copy(bf16[128,128]{1,0:T(8,128)(2,1)S(1)} %get-tuple-element.26) | data formatting | bytes 65536
